TPU v7x, 32 devices: a whole 2x2x4 slice. The times are simulated.
32 devices in a mesh: grp: 2 (over y), src: 4 (over z), snk: 4 (over x, core).
Axes of the slice: x: 2, y: 2, z: 4, core: 2. Of those that a mesh axis runs over, the one named last changes fastest.
Arguments:
- solutions: bfloat16 [8, 4, 2, 4, 64, 3, 128], P(('grp', 'src'), None, None, None, 'snk'), parts along dimension 0, may hold values from -6 to 6
- eigvecs: bfloat16 [8, 2, 64, 3, 512], P(('grp', 'snk')), parts along dimension 0, may hold values from -0.3125 to 0.3125
- momenta: int32 [8, 3], replicated, may hold values from -2 to 2
- ordering: int32 [512], replicated, may hold values from 0 to 511, each once
Outputs:
- peramb: bfloat16 [8, 4, 2, 512, 4, 128], P(('grp', 'snk'), 'src'), parts along dimension 0
- correlator: float32 [8, 4, 2, 8], P(('grp', 'snk'), 'src'), parts along dimension 0
There are 2 independent parts, one for each index of `grp`. A program takes and returns all parts, laid end to end along the dimension named above; an argument that names none is the same for every part. Nothing has to cross between parts.
Inputs may be any that keep to these rules, and one draw needn't show every extreme that they name: `momenta`: components in units of 2 pi / 64; the third (z) has no effect on the window. `ordering`: each eigenvector index once.
All inputs are finite; a program needn't handle non-finite values.
Results may differ from a plain program's by a relative error of at most 0.0034.
Values may be sent and summed in bfloat16 or wider, within the bound.
A program may use at most 64 MiB of HBM per device.

v0:
```python
import math

import jax
import jax.numpy as jnp
from jax import lax
from jax.sharding import PartitionSpec as P

NEV = 512
WINDOW_SITES = 64
LAT = 64
NB = 32


PRECISE = lax.Precision.HIGHEST
SPIN_SIGNS = (1.0, 1.0, -1.0, -1.0)


def broadcast(block, axis, owner):
    block = jnp.where(lax.axis_index(axis) == owner, block, jnp.zeros_like(block))
    return lax.psum(block, axis)


def einsum_half(form, *operands):
    return jnp.einsum(form, *operands, preferred_element_type=jnp.float32)


def einsum_full(form, *operands):
    return jnp.einsum(form, *operands, precision=PRECISE)


def phase_tables(momenta):
    lattice_site_index = jnp.arange(WINDOW_SITES, dtype=jnp.int32)
    coord_x = (lattice_site_index % LAT).astype(jnp.float32)
    coord_y = (lattice_site_index // LAT % LAT).astype(jnp.float32)
    coord_z = (lattice_site_index // (LAT * LAT)).astype(jnp.float32)
    momentum_f = momenta.astype(jnp.float32)
    phase_angle = (
        2.0
        * math.pi
        / LAT
        * (
            momentum_f[:, 0:1] * coord_x[None, :]
            + momentum_f[:, 1:2] * coord_y[None, :]
            + momentum_f[:, 2:3] * coord_z[None, :]
        )
    )
    return (jnp.cos(phase_angle), jnp.sin(phase_angle))


def block_onehot(ordering):
    block_ids = jnp.arange(NB, dtype=jnp.int32)
    return (ordering[:, None] // (NEV // NB) == block_ids[None, :]).astype(jnp.bfloat16)


def block_factors(eigen, onehot):
    return einsum_half("rxck,kb->rxcb", eigen, onehot)


def elementals_from(factors, phase_cos, phase_sine_part):
    fac_real, fac_imag = (factors[0], factors[1])
    pair_real = einsum_full("xce,xcb->xeb", fac_real, fac_real) + einsum_full(
        "xce,xcb->xeb", fac_imag, fac_imag
    )
    pairing_imaginary = einsum_full("xce,xcb->xeb", fac_real, fac_imag) - einsum_full(
        "xce,xcb->xeb", fac_imag, fac_real
    )
    elemental_real = einsum_full("px,xeb->peb", phase_cos, pair_real) + einsum_full(
        "px,xeb->peb", phase_sine_part, pairing_imaginary
    )
    elem_imag = einsum_full("px,xeb->peb", phase_cos, pairing_imaginary) - einsum_full(
        "px,xeb->peb", phase_sine_part, pair_real
    )
    return jnp.stack([elemental_real, elem_imag])


def project(eigen, solution):
    eig_real, eig_imag = (eigen[0], eigen[1])
    sol_real, sol_imag = (solution[0], solution[1])
    tau_real = einsum_half("xck,axcd->kad", eig_real, sol_real) + einsum_half(
        "xck,axcd->kad", eig_imag, sol_imag
    )
    tau_imag = einsum_half("xck,axcd->kad", eig_real, sol_imag) - einsum_half(
        "xck,axcd->kad", eig_imag, sol_real
    )
    return jnp.stack([tau_real, tau_imag]).astype(jnp.bfloat16)


def correlate(eigen, peramb, phase_cos, phase_sine_part, elementals):
    eig_real, eig_imag = (eigen[0], eigen[1])
    smear_real = einsum_half("xck,kad->axcd", eig_real, peramb[0]) - einsum_half(
        "xck,kad->axcd", eig_imag, peramb[1]
    )
    smear_imag = einsum_half("xck,kad->axcd", eig_real, peramb[1]) + einsum_half(
        "xck,kad->axcd", eig_imag, peramb[0]
    )
    smear_real = smear_real.reshape(4, WINDOW_SITES, 3, 4, NB)
    smear_imag = smear_imag.reshape(4, WINDOW_SITES, 3, 4, NB)
    spin_sign = jnp.array(SPIN_SIGNS, dtype=jnp.float32)
    loop_real = einsum_full("a,axcsb,axcse->xbe", spin_sign, smear_real, smear_real) + einsum_full(
        "a,axcsb,axcse->xbe", spin_sign, smear_imag, smear_imag
    )
    loop_imag = einsum_full("a,axcsb,axcse->xbe", spin_sign, smear_real, smear_imag) - einsum_full(
        "a,axcsb,axcse->xbe", spin_sign, smear_imag, smear_real
    )
    sink_real = einsum_full("px,xbe->pbe", phase_cos, loop_real) - einsum_full(
        "px,xbe->pbe", phase_sine_part, loop_imag
    )
    sink_imag = einsum_full("px,xbe->pbe", phase_cos, loop_imag) + einsum_full(
        "px,xbe->pbe", phase_sine_part, loop_real
    )
    src_real, src_imag = (elementals[0], elementals[1])
    corr_real = einsum_full("pbe,peb->p", sink_real, src_real) - einsum_full(
        "pbe,peb->p", sink_imag, src_imag
    )
    corr_imag = einsum_full("pbe,peb->p", sink_real, src_imag) + einsum_full(
        "pbe,peb->p", sink_imag, src_real
    )
    return jnp.stack([corr_real, corr_imag]) * (1.0 / (WINDOW_SITES * NB))


def body(solutions, eigvecs, momenta, ordering):
    eigen = eigvecs[0]
    phase_cos, phase_sine_part = phase_tables(momenta)
    onehot = block_onehot(ordering)
    own_elementals = elementals_from(block_factors(eigen, onehot), phase_cos, phase_sine_part)
    elementals = broadcast(own_elementals, "snk", lax.axis_index("src"))
    arrived = lax.all_to_all(solutions, "snk", split_axis=1, concat_axis=4, tiled=True)
    peramb = project(eigen, arrived[0, 0])
    correlator = correlate(eigen, peramb, phase_cos, phase_sine_part, elementals)
    return (peramb[None, None], correlator[None, None])


def solution(mesh):
    return jax.shard_map(
        body,
        mesh=mesh,
        in_specs=(
            P(("grp", "src"), None, None, None, "snk", None, None),
            P(("grp", "snk"), None, None, None, None),
            P(),
            P(),
        ),
        out_specs=(
            P(("grp", "snk"), "src", None, None, None, None),
            P(("grp", "snk"), "src", None, None),
        ),
        check_vma=False,
    )
```

profile of v0, /device:TPU:17, one launch (start us, length us, event | category | flops | bytes accessed | tf_op | source)
XLA Modules:
  0.0 86.7 jit_solution(2492704756171456559)
XLA Ops:
  7.2 4.1 %all-to-all-start = ((bf16[1,4,2,4,16,3,128]{6,4,5,3,2,0,1:T(8,128)(2,1)}), bf16[1,4,2,4,16,3,128]{6,4,5,3,2,0,1:T(8,128)(2,1)S(1)}, u32[]{:S(2)}, u32[]{:S(2)}) async-start(bf16[1,4,2,4,16,3,128]{6,4,5,3,2,0,1:T(8,128)(2,1)} %bitcast.195), calls=%async_computation | async-start | bytes 786432 | tf_op jit(solution)/shard_map/all_to_all | solution.py:127
  14.2 1.8 %fusion.129 = f32[64,32,32]{2,1,0:T(8,128)S(1)} fusion(f32[64,3,32]{2,1,0:T(4,128)S(1)} %copy.76), kind=kOutput, calls=%fused_computation.173 | convolution fusion | flops 2359296 | bytes 286720 | tf_op jit(solution)/shard_map/xce,xcb->xeb/dot_general | solution.py:28
  16.0 1.8 %fusion.130 = f32[64,32,32]{2,1,0:T(8,128)S(1)} fusion(f32[64,3,32]{2,1,0:T(4,128)S(1)} %copy.76, f32[64,3,32]{2,1,0:T(4,128)S(1)} %copy.78), kind=kOutput, calls=%fused_computation.174 | convolution fusion | flops 2359296 | bytes 311296 | tf_op jit(solution)/shard_map/xce,xcb->xeb/dot_general | solution.py:28
  17.9 1.8 %convolution_subtract_fusion = f32[64,32,32]{2,1,0:T(8,128)S(1)} fusion(f32[64,32,32]{2,1,0:T(8,128)S(1)} %fusion.130, f32[64,3,32]{2,1,0:T(4,128)S(1)} %copy.78, f32[64,3,32]{2,1,0:T(4,128)S(1)} %copy.76), kind=kOutput, calls=%fused_computation.4 | convolution fusion | flops 2424832 | bytes 573440 | tf_op jit(solution)/shard_map/xce,xcb->xeb/dot_general | solution.py:28
  20.3 1.8 %convolution_add_fusion = f32[64,32,32]{2,1,0:T(8,128)S(1)} fusion(f32[64,32,32]{2,1,0:T(8,128)S(1)} %fusion.129, f32[64,3,32]{2,1,0:T(4,128)S(1)} %copy.78), kind=kOutput, calls=%fused_computation.5 | convolution fusion | flops 2424832 | bytes 548864 | tf_op jit(solution)/shard_map/xce,xcb->xeb/dot_general | solution.py:28
  22.8 2.2 %fusion.42 = f32[8,32,32]{2,0,1:T(8,128)S(1)} fusion(f32[64,32,32]{0,2,1:T(8,128)S(1)} %copy.85, f32[64]{0:T(128)S(1)} %get-tuple-element.23, f32[8]{0:T(128)S(1)} %get-tuple-element.19, f32[64]{0:T(128)S(1)} %fusion.118, f32[8]{0:T(128)S(1)} %get-tuple-element.20, f32[64]{0:T(128)S(1)} %get-tuple-element.24, f32[8]{0:T(128)S(1)} %get-tuple-element.18), kind=kOutput, calls=%fused_computation.71 | convolution fusion | flops 6294528 | bytes 295776 | tf_op jit(solution)/shard_map/px,xeb->peb/dot_general | solution.py:28
  25.0 2.2 %fusion.44 = f32[8,32,32]{2,0,1:T(8,128)S(1)} fusion(f32[64,32,32]{0,2,1:T(8,128)S(1)} %copy.80, f32[64]{0:T(128)S(1)} %get-tuple-element.23, f32[8]{0:T(128)S(1)} %get-tuple-element.19, f32[64]{0:T(128)S(1)} %fusion.118, f32[8]{0:T(128)S(1)} %get-tuple-element.20, f32[64]{0:T(128)S(1)} %get-tuple-element.24, f32[8]{0:T(128)S(1)} %get-tuple-element.18), kind=kOutput, calls=%fused_computation.73 | convolution fusion | flops 6294528 | bytes 295776 | tf_op jit(solution)/shard_map/px,xeb->peb/dot_general | solution.py:28
  27.2 2.2 %fusion.8 = f32[1,8,32,32]{3,1,2,0:T(8,128)S(1)} fusion(f32[8,32,32]{2,0,1:T(8,128)S(1)} %fusion.42, f32[64,32,32]{0,2,1:T(8,128)S(1)} %copy.80, f32[64]{0:T(128)S(1)} %get-tuple-element.23, f32[8]{0:T(128)S(1)} %get-tuple-element.19, f32[64]{0:T(128)S(1)} %fusion.118, f32[8]{0:T(128)S(1)} %get-tuple-element.20, f32[64]{0:T(128)S(1)} %get-tuple-element.24, ...), kind=kOutput, calls=%fused_computation.22 | convolution fusion | flops 6302720 | bytes 328544 | tf_op jit(solution)/shard_map/px,xeb->peb/dot_general | solution.py:28
  29.4 2.2 %fusion.9 = f32[1,8,32,32]{3,1,2,0:T(8,128)S(1)} fusion(f32[8,32,32]{2,0,1:T(8,128)S(1)} %fusion.44, f32[64,32,32]{0,2,1:T(8,128)S(1)} %copy.85, f32[64]{0:T(128)S(1)} %get-tuple-element.23, f32[8]{0:T(128)S(1)} %get-tuple-element.19, f32[64]{0:T(128)S(1)} %fusion.118, f32[8]{0:T(128)S(1)} %get-tuple-element.20, f32[64]{0:T(128)S(1)} %get-tuple-element.24, ...), kind=kOutput, calls=%fused_computation.24 | convolution fusion | flops 6302720 | bytes 328544 | tf_op jit(solution)/shard_map/px,xeb->peb/dot_general | solution.py:28
  35.7 1.6 %copy.69 = f32[4,64,3,4,32]{4,3,2,0,1:T(4,128)} copy(f32[4,64,3,4,32]{1,4,3,2,0:T(8,128)S(1)} %bitcast.188) | data formatting | bytes 786432 | tf_op jit(solution)/shard_map/reshape | solution.py:97
  37.3 1.6 %copy.66 = f32[4,64,3,4,32]{4,3,2,0,1:T(4,128)} copy(f32[4,64,3,4,32]{1,4,3,2,0:T(8,128)S(1)} %bitcast.186) | data formatting | bytes 786432 | tf_op jit(solution)/shard_map/reshape | solution.py:96
  40.3 2.6 %copy.68 = f32[4,64,3,4,32]{4,3,2,0,1:T(4,128)} copy(f32[4,64,3,4,32]{1,4,3,2,0:T(8,128)} %get-tuple-element.22) | data formatting | bytes 786432 | tf_op jit(solution)/shard_map/a,axcsb,axcse->xbe/dot_general | solution.py:28
  42.9 1.6 %copy.65 = f32[4,64,3,4,32]{4,3,2,0,1:T(4,128)} copy(f32[4,64,3,4,32]{1,4,3,2,0:T(8,128)S(1)} %copy-done.1) | data formatting | bytes 786432 | tf_op jit(solution)/shard_map/a,axcsb,axcse->xbe/dot_general | solution.py:28
  44.5 4.9 %convolution_bitcast_fusion.6 = f32[64,32,32]{2,1,0:T(8,128)S(1)} fusion(f32[4,64,3,4,32]{4,3,2,0,1:T(4,128)} %copy.68, f32[4,64,3,4,32]{4,3,2,0,1:T(4,128)} %copy.69), kind=kOutput, calls=%fused_computation.8 | convolution fusion | flops 37748736 | bytes 1048576 | tf_op jit(solution)/shard_map/a,axcsb,axcse->xbe/dot_general | solution.py:28
  49.5 4.0 %convolution_bitcast_fusion.4 = f32[64,32,32]{2,1,0:T(8,128)} fusion(f32[4,64,3,4,32]{4,3,2,0,1:T(4,128)S(1)} %copy-done.5, f32[4,64,3,4,32]{4,3,2,0,1:T(4,128)S(1)} %copy-done.3), kind=kOutput, calls=%fused_computation.6 | convolution fusion | flops 37748736 | bytes 1048576 | tf_op jit(solution)/shard_map/a,axcsb,axcse->xbe/dot_general | solution.py:28
  53.5 4.1 %fusion.2 = f32[64,32,32]{2,1,0:T(8,128)} fusion(f32[64,32,32]{2,1,0:T(8,128)S(1)} %convolution_bitcast_fusion.6, f32[4,64,3,4,32]{4,3,2,0,1:T(4,128)S(1)} %copy-done.4, f32[4,64,3,4,32]{4,3,2,0,1:T(4,128)S(1)} %copy-done.3), kind=kOutput, calls=%fused_computation.12 | convolution fusion | flops 37814272 | bytes 1310720 | tf_op jit(solution)/shard_map/a,axcsb,axcse->xbe/dot_general | solution.py:28
  57.6 1.9 %copy.70 = f32[64,32,32]{0,2,1:T(8,128)S(1)} copy(f32[64,32,32]{2,1,0:T(8,128)} %fusion.2) | data formatting | bytes 524288 | tf_op jit(solution)/shard_map/add | solution.py:99
  59.5 2.2 %fusion.46 = f32[8,32,32]{2,0,1:T(8,128)S(1)} fusion(f32[64,32,32]{0,2,1:T(8,128)S(1)} %copy.70, f32[64]{0:T(128)S(1)} %get-tuple-element.23, f32[8]{0:T(128)S(1)} %get-tuple-element.19, f32[64]{0:T(128)S(1)} %copy-done.10, f32[8]{0:T(128)S(1)} %get-tuple-element.20, f32[64]{0:T(128)S(1)} %copy-done.7, f32[8]{0:T(128)S(1)} %get-tuple-element.18), kind=kOutput, calls=%fused_computation.75 | convolution fusion | flops 6294528 | bytes 295776 | tf_op jit(solution)/shard_map/px,xbe->pbe/dot_general | solution.py:28
  61.7 5.9 %fusion.3 = f32[64,32,32]{2,1,0:T(8,128)} fusion(f32[64,32,32]{2,1,0:T(8,128)} %convolution_bitcast_fusion.4, f32[4,64,3,4,32]{4,3,2,0,1:T(4,128)} %copy.65, f32[4,64,3,4,32]{4,3,2,0,1:T(4,128)S(1)} %copy-done.2), kind=kOutput, calls=%fused_computation.13 | convolution fusion | flops 37814272 | bytes 1310720 | tf_op jit(solution)/shard_map/a,axcsb,axcse->xbe/dot_general | solution.py:28
  67.5 1.8 %copy.75 = f32[64,32,32]{0,2,1:T(8,128)S(1)} copy(f32[64,32,32]{2,1,0:T(8,128)} %fusion.3) | data formatting | bytes 524288 | tf_op jit(solution)/shard_map/sub | solution.py:102
  69.3 2.2 %fusion.40 = f32[8,32,32]{2,0,1:T(8,128)S(1)} fusion(f32[64,32,32]{0,2,1:T(8,128)S(1)} %copy.75, f32[64]{0:T(128)S(1)} %get-tuple-element.23, f32[8]{0:T(128)S(1)} %get-tuple-element.19, f32[64]{0:T(128)S(1)} %copy-done.10, f32[8]{0:T(128)S(1)} %get-tuple-element.20, f32[64]{0:T(128)S(1)} %copy-done.7, f32[8]{0:T(128)S(1)} %get-tuple-element.18), kind=kOutput, calls=%fused_computation.69 | convolution fusion | flops 6294528 | bytes 295776 | tf_op jit(solution)/shard_map/px,xbe->pbe/dot_general | solution.py:28
  71.5 2.2 %convolution_subtract_fusion.3 = f32[8,32,32]{2,0,1:T(8,128)S(1)} fusion(f32[8,32,32]{2,0,1:T(8,128)S(1)} %fusion.46, f32[64,32,32]{0,2,1:T(8,128)S(1)} %copy.75, f32[64]{0:T(128)S(1)} %get-tuple-element.23, f32[8]{0:T(128)S(1)} %get-tuple-element.19, f32[64]{0:T(128)S(1)} %copy-done.10, f32[8]{0:T(128)S(1)} %get-tuple-element.20, f32[64]{0:T(128)S(1)} %copy-done.7, ...), kind=kOutput, calls=%fused_computation.25 | convolution fusion | flops 6302720 | bytes 328544 | tf_op jit(solution)/shard_map/px,xbe->pbe/dot_general | solution.py:28
  73.7 2.2 %convolution_add_fusion.2 = f32[8,32,32]{2,0,1:T(8,128)S(1)} fusion(f32[8,32,32]{2,0,1:T(8,128)S(1)} %fusion.40, f32[64,32,32]{0,2,1:T(8,128)S(1)} %copy.70, f32[64]{0:T(128)S(1)} %get-tuple-element.23, f32[8]{0:T(128)S(1)} %get-tuple-element.19, f32[64]{0:T(128)S(1)} %copy-done.11, f32[8]{0:T(128)S(1)} %get-tuple-element.20, f32[64]{0:T(128)S(1)} %copy-done.8, ...), kind=kOutput, calls=%fused_computation.20 | convolution fusion | flops 6302720 | bytes 328544 | tf_op jit(solution)/shard_map/px,xbe->pbe/dot_general | solution.py:28
  76.3 1.8 %copy.90 = bf16[1,1,2,512,4,128]{5,4,3,2,1,0:T(4,128)(2,1)} copy(bf16[1,1,2,512,4,128]{5,3,4,2,1,0:T(8,128)(2,1)S(1)} %pad_maximum_fusion) | data formatting | bytes 2097152
  (63 shorter events, 11.6 us)
Async XLA Ops:
  7.2 25.2 %all-to-all-start = ((bf16[1,4,2,4,16,3,128]{6,4,5,3,2,0,1:T(8,128)(2,1)}), bf16[1,4,2,4,16,3,128]{6,4,5,3,2,0,1:T(8,128)(2,1)S(1)}, u32[]{:S(2)}, u32[]{:S(2)}) async-start(bf16[1,4,2,4,16,3,128]{6,4,5,3,2,0,1:T(8,128)(2,1)} %bitcast.195), calls=%async_computation | async-start | bytes 786432 | tf_op jit(solution)/shard_map/all_to_all | solution.py:127
  11.3 66.8 %all-reduce.2.cloned.1.call-start = ((), (), s32[]{:S(2)}) async-start(), calls=%async_computation.1 | async-start | bytes 524288 | tf_op jit(solution)/shard_map/psum | solution.py:20
  11.3 18.1 %copy-start.6 = (f32[64]{0:T(128)}, f32[64]{0:T(128)S(1)}, u32[]{:S(2)}) copy-start(f32[64]{0:T(128)S(1)} %get-tuple-element.24) | copy-start | bytes 772
  11.3 18.1 %copy-start.9 = (f32[64]{0:T(128)}, f32[64]{0:T(128)S(1)}, u32[]{:S(2)}) copy-start(f32[64]{0:T(128)S(1)} %fusion.118) | copy-start | bytes 772
  29.4 3.1 %copy-start = (bf16[1,2,64,3,512]{4,2,3,1,0:T(8,128)(2,1)S(1)}, bf16[1,2,64,3,512]{4,2,3,1,0:T(8,128)(2,1)}, u32[]{:S(2)}) copy-start(bf16[1,2,64,3,512]{4,2,3,1,0:T(8,128)(2,1)} %param.6) | copy-start | bytes 1179652
  37.3 1.6 %copy-start.12 = (f32[4]{0:T(128)S(1)}, f32[4]{0:T(128)}, u32[]{:S(2)}) copy-start(f32[4]{0:T(128)} %constant.77.clone) | copy-start | bytes 52
  40.3 2.6 %copy-start.1 = (f32[4,64,3,4,32]{1,4,3,2,0:T(8,128)S(1)}, f32[4,64,3,4,32]{1,4,3,2,0:T(8,128)}, u32[]{:S(2)}) copy-start(f32[4,64,3,4,32]{1,4,3,2,0:T(8,128)} %get-tuple-element.21) | copy-start | bytes 1179652
  44.5 5.0 %copy-start.3 = (f32[4,64,3,4,32]{4,3,2,0,1:T(4,128)S(1)}, f32[4,64,3,4,32]{4,3,2,0,1:T(4,128)}, u32[]{:S(2)}) copy-start(f32[4,64,3,4,32]{4,3,2,0,1:T(4,128)} %copy.66) | copy-start | bytes 1179652
  44.5 5.0 %copy-start.5 = (f32[4,64,3,4,32]{4,3,2,0,1:T(4,128)S(1)}, f32[4,64,3,4,32]{4,3,2,0,1:T(4,128)}, u32[]{:S(2)}) copy-start(f32[4,64,3,4,32]{4,3,2,0,1:T(4,128)} %copy.68) | copy-start | bytes 1179652
  49.5 4.0 %copy-start.4 = (f32[4,64,3,4,32]{4,3,2,0,1:T(4,128)S(1)}, f32[4,64,3,4,32]{4,3,2,0,1:T(4,128)}, u32[]{:S(2)}) copy-start(f32[4,64,3,4,32]{4,3,2,0,1:T(4,128)} %copy.65) | copy-start | bytes 1179652
  53.5 6.0 %copy-start.7 = (f32[64]{0:T(128)S(1)}, f32[64]{0:T(128)}, u32[]{:S(2)}) copy-start(f32[64]{0:T(128)} %copy-done.6) | copy-start | bytes 772
  53.5 6.0 %copy-start.10 = (f32[64]{0:T(128)S(1)}, f32[64]{0:T(128)}, u32[]{:S(2)}) copy-start(f32[64]{0:T(128)} %copy-done.9) | copy-start | bytes 772
  57.6 4.1 %copy-start.2 = (f32[4,64,3,4,32]{4,3,2,0,1:T(4,128)S(1)}, f32[4,64,3,4,32]{4,3,2,0,1:T(4,128)}, u32[]{:S(2)}) copy-start(f32[4,64,3,4,32]{4,3,2,0,1:T(4,128)} %copy.69) | copy-start | bytes 1179652
  67.5 6.2 %copy-start.8 = (f32[64]{0:T(128)S(1)}, f32[64]{0:T(128)}, u32[]{:S(2)}) copy-start(f32[64]{0:T(128)} %copy-done.6) | copy-start | bytes 772
  67.5 6.2 %copy-start.11 = (f32[64]{0:T(128)S(1)}, f32[64]{0:T(128)}, u32[]{:S(2)}) copy-start(f32[64]{0:T(128)} %copy-done.9) | copy-start | bytes 772
Sparse Core Ops, SparseCore 0:
  32.5 31.7 all-reduce.1
where the time goes:
time: 87.3 us; the launch traced here: 86.7 us
  matrix products  47.7 us (55%)
  local copies, waits for them, and re-layouts  15.1 us (17%)
  between operations  14.3 us (16%)
  other arithmetic  5.46 us (6%)
  starting transfers between devices  4.11 us (5%)
    dot_general x16, matrix products, einsum_full(): return jnp.einsum(form, *operands, precision=PRECISE)  43.9 us
    dot_general x2, local copies, waits for them, and re-layouts, einsum_full(): return jnp.einsum(form, *operands, precision=PRECISE)  4.18 us
    all_to_all x1, starting transfers between devices, body(): lax.all_to_all(solutions, 'snk', split_axis=1, concat_axis=4, tiled=True)  4.11 us
    dot_general x9, matrix products, einsum_half(): return jnp.einsum(form, *operands, preferred_element_type=jnp.float32)  3.84 us
    dot_general x2, other arithmetic, einsum_full(): return jnp.einsum(form, *operands, precision=PRECISE)  2.61 us
    unnamed x29, local copies, waits for them, and re-layouts  2.09 us
    add x1, local copies, waits for them, and re-layouts, correlate(): einsum_full('a,axcsb,axcse->xbe', spin_sign, smear_real, smear_real)  1.89 us
    sub x1, local copies, waits for them, and re-layouts, correlate(): einsum_full('a,axcsb,axcse->xbe', spin_sign, smear_real, smear_imag)  1.78 us
  transfers between devices with their start and end apart: 2, of which 0 were waited for; matrix products, arithmetic and copies ran while one was open for 77% of the time, Pallas kernels for 0%

commit v1 on v0

v1 whole, which is shorter than its diff:
```python
import functools
import math

import jax
import jax.numpy as jnp
import numpy as np
from jax import lax
from jax.experimental import pallas as pl
from jax.experimental.pallas import tpu as pltpu
from jax.sharding import PartitionSpec as P

LAT = 64
NB = 32
SPIN_SIGNS = (1.0, 1.0, -1.0, -1.0)
EXACT = lax.Precision.HIGHEST
MESH = pl.DeviceIdType.MESH


def site_coordinates(peers, rows, colours, local):
    table = np.zeros((8, peers, rows), np.int32)
    for owner in range(peers):
        for colour in range(colours):
            site = owner * local + np.arange(local)
            here = slice(colour * local, (colour + 1) * local)
            table[0, owner, here] = site % LAT
            table[1, owner, here] = site // LAT % LAT
            table[2, owner, here] = site // (LAT * LAT)
    table = table.reshape(8, peers * rows)
    return np.concatenate([table, table], axis=1)


def split(values):
    high = values.astype(jnp.bfloat16).astype(jnp.float32)
    return high, values - high


def kernel(
    dims, momenta_ref, ordering_ref, coords_ref, eig_hbm, sol_hbm, peramb_ref, corr_ref,
    eig, eig_t, sol, pairs, fac_own, fac_got, table, weights,
    eig_sem, sol_sem, send_sem, recv_sem, fac_send, fac_recv,
):
    peers, spins, rows, local, colours, nev, dil, moms, direct, scale = dims
    total = peers * rows
    me = lax.axis_index("snk")
    source = lax.axis_index("src")

    if direct:
        eig_copies = [
            pltpu.make_async_copy(
                eig_hbm.at[:, c, j],
                eig.at[:, j, pl.ds(c * local, local)],
                eig_sem.at[j * colours + c],
            )
            for j in range(peers)
            for c in range(colours)
        ]
    else:
        eig_copies = [pltpu.make_async_copy(eig_hbm, eig, eig_sem.at[0])]
    own_copies = [
        pltpu.make_async_copy(sol_hbm.at[me, :, a], sol.at[a, :, me], sol_sem.at[a])
        for a in range(spins)
    ]
    for copy in eig_copies + own_copies:
        copy.start()

    barrier = pltpu.get_barrier_semaphore()
    for d in range(1, peers):
        other = lax.rem(me + d, peers)
        pl.semaphore_signal(barrier, inc=1, device_id={"snk": other}, device_id_type=MESH)
    pl.semaphore_wait(barrier, peers - 1)

    sends = []
    for a in range(spins):
        for d in range(1, peers):
            other = lax.rem(me + d, peers)
            copy = pltpu.make_async_remote_copy(
                src_ref=sol_hbm.at[other, :, a],
                dst_ref=sol.at[a, :, me],
                send_sem=send_sem.at[a, d],
                recv_sem=recv_sem.at[a, d],
                device_id={"snk": other},
                device_id_type=MESH,
            )
            copy.start()
            sends.append(copy)

    for copy in eig_copies:
        copy.wait()
    vectors = eig[...].reshape(2 * total, nev)
    block_of = lax.div(ordering_ref[...], jnp.int32(nev // NB))
    onehot = (block_of == lax.broadcasted_iota(jnp.int32, (NB, nev), 0)).astype(jnp.bfloat16)
    fac_own[...] = lax.dot_general(
        onehot, vectors, (((1,), (1,)), ((), ())), preferred_element_type=jnp.float32
    )

    fac_sends = []
    for d in range(1, peers):
        other = lax.rem(me + d, peers)
        fac_sends.append(
            pltpu.make_async_remote_copy(
                src_ref=fac_own,
                dst_ref=fac_got,
                send_sem=fac_send.at[d],
                recv_sem=fac_recv,
                device_id={"snk": other},
                device_id_type=MESH,
            )
        )

    @pl.when(me == source)
    def _():
        for copy in fac_sends:
            copy.start()

    eig_t[...] = vectors.astype(jnp.float32).T.astype(jnp.bfloat16)

    mom = [jnp.zeros((moms, 2 * total), jnp.int32) for _ in range(3)]
    which = lax.broadcasted_iota(jnp.int32, (moms, 2 * total), 0)
    for i in range(3):
        for p in range(moms):
            mom[i] = jnp.where(which == p, momenta_ref[p, i], mom[i])
    turns = sum(mom[i] * coords_ref[i : i + 1, :] for i in range(3))
    turns = jnp.bitwise_and(turns + LAT // 2, LAT - 1) - LAT // 2
    angle = turns.astype(jnp.float32) * (2.0 * math.pi / LAT)
    phases = jnp.concatenate([jnp.cos(angle), jnp.sin(angle)], axis=0)

    def smear(a):
        own_copies[a].wait()
        for copy in sends[a * (peers - 1) : (a + 1) * (peers - 1)]:
            copy.wait_recv()
        s_real = sol[a, 0].reshape(total, dil)
        s_imag = sol[a, 1].reshape(total, dil)
        right = jnp.concatenate(
            [
                jnp.concatenate([s_real, s_imag], axis=1),
                jnp.concatenate([s_imag, -s_real], axis=1),
            ],
            axis=0,
        )
        projected = jnp.dot(eig_t[...], right, preferred_element_type=jnp.float32)
        pairs[pl.ds(a, nev, stride=spins), :] = projected[:, :dil]
        pairs[pl.ds(nev * spins + a, nev, stride=spins), :] = projected[:, dil:]
        full = jnp.dot(
            eig[...].reshape(2 * total, nev),
            projected.astype(jnp.bfloat16),
            preferred_element_type=jnp.float32,
        )
        real = full[:total, :dil] - full[total:, dil:]
        imag = full[:total, dil:] + full[total:, :dil]
        return jnp.concatenate([real, imag], axis=1).T

    def correlate(a, smeared):
        high, low = split(smeared)
        high, low = high.astype(jnp.bfloat16), low.astype(jnp.bfloat16)
        part = jnp.zeros((2 * total, total), jnp.float32)
        for sigma in range(dil // NB):
            r, i = sigma * NB, dil + sigma * NB
            right = jnp.concatenate(
                [
                    high[r : r + NB], high[i : i + NB],
                    low[r : r + NB], low[i : i + NB],
                    high[r : r + NB], high[i : i + NB],
                ],
                axis=0,
            )
            g = jnp.dot(table[...], right, preferred_element_type=jnp.float32)
            part = part + g * g
        if a == 0:
            weights[...] = part * SPIN_SIGNS[a]
        elif SPIN_SIGNS[a] > 0:
            weights[...] += part
        else:
            weights[...] -= part

    first = smear(0)

    @pl.when(me != source)
    def _():
        fac_sends[0].wait_recv()

    @pl.when(me == source)
    def _():
        fac_got[...] = fac_own[...]

    got = fac_got[...]
    sign = jnp.where(lax.broadcasted_iota(jnp.int32, got.shape, 1) < total, 1.0, -1.0)
    swapped = pltpu.roll(got, total, 1)
    high, low = split(jnp.concatenate([got * sign, swapped], axis=0))
    table[...] = jnp.concatenate([high, high, low], axis=0).T.astype(jnp.bfloat16)

    correlate(0, first)
    for a in range(1, spins):
        correlate(a, smear(a))
    peramb_ref[...] = pairs[...].astype(jnp.bfloat16)

    summed = lax.dot_general(
        phases, weights[...], (((1,), (0,)), ((), ())),
        precision=EXACT, preferred_element_type=jnp.float32,
    )
    at_cos, at_sin = phases[:moms, :total], phases[moms:, :total]
    sum_cos, sum_sin = summed[:moms], summed[moms:]
    real = jnp.sum(at_cos * sum_cos + at_sin * sum_sin, axis=1, keepdims=True)
    imag = jnp.sum(at_sin * sum_cos - at_cos * sum_sin, axis=1, keepdims=True)
    square = (moms, moms)
    eye = lax.broadcasted_iota(jnp.int32, square, 0) == lax.broadcasted_iota(jnp.int32, square, 1)
    out = [
        jnp.sum(jnp.where(eye, column, 0.0), axis=0, keepdims=True) * scale
        for column in (real, imag)
    ]
    corr_ref[...] = jnp.concatenate(out, axis=0)

    for copy in sends:
        copy.wait_send()

    @pl.when(me == source)
    def _():
        for copy in fac_sends:
            copy.wait_send()


def body(peers, solutions, eigvecs, momenta, ordering):
    _, times, _, spins, local, colours, dil = solutions.shape
    sites, nev = eigvecs.shape[2], eigvecs.shape[4]
    moms = momenta.shape[0]
    used = colours * local
    rows = -(-used // 16) * 16
    direct = local % 16 == 0
    total = peers * rows

    sol = jnp.transpose(solutions[0], (0, 1, 2, 4, 3, 5)).reshape(times, 2, spins, used, dil)
    eig = jnp.transpose(eigvecs[0], (0, 2, 1, 3)).reshape(2, colours, peers, local, nev)
    if not direct:
        pad = ((0, 0), (0, 0), (0, 0), (0, rows - used), (0, 0))
        sol = jnp.pad(sol, pad)
        eig = jnp.transpose(eig, (0, 2, 1, 3, 4)).reshape(2, peers, used, nev)
        eig = jnp.pad(eig, pad[1:])
    coords = jnp.asarray(site_coordinates(peers, rows, colours, local))
    scale = 1.0 / (sites * NB)

    vmem = pl.BlockSpec(memory_space=pltpu.VMEM)
    dims = (peers, spins, rows, local, colours, nev, dil, moms, direct, scale)
    peramb, corr = pl.pallas_call(
        functools.partial(kernel, dims),
        out_shape=(
            jax.ShapeDtypeStruct((2 * nev * spins, dil), jnp.bfloat16),
            jax.ShapeDtypeStruct((2, moms), jnp.float32),
        ),
        in_specs=[
            pl.BlockSpec(memory_space=pltpu.SMEM),
            vmem,
            vmem,
            pl.BlockSpec(memory_space=pl.ANY),
            pl.BlockSpec(memory_space=pl.ANY),
        ],
        out_specs=(vmem, vmem),
        scratch_shapes=[
            pltpu.VMEM((2, peers, rows, nev), jnp.bfloat16),
            pltpu.VMEM((nev, 2 * total), jnp.bfloat16),
            pltpu.VMEM((spins, 2, peers, rows, dil), jnp.bfloat16),
            pltpu.VMEM((2 * nev * spins, dil), jnp.float32),
            pltpu.VMEM((NB, 2 * total), jnp.float32),
            pltpu.VMEM((NB, 2 * total), jnp.float32),
            pltpu.VMEM((2 * total, 6 * NB), jnp.bfloat16),
            pltpu.VMEM((2 * total, total), jnp.float32),
            pltpu.SemaphoreType.DMA((peers * colours,)),
            pltpu.SemaphoreType.DMA((spins,)),
            pltpu.SemaphoreType.DMA((spins, peers)),
            pltpu.SemaphoreType.DMA((spins, peers)),
            pltpu.SemaphoreType.DMA((peers,)),
            pltpu.SemaphoreType.DMA,
        ],
        compiler_params=pltpu.CompilerParams(
            collective_id=0, has_side_effects=True, vmem_limit_bytes=40 * 1024 * 1024
        ),
    )(momenta, ordering.reshape(1, nev), coords, eig, sol)
    return peramb.reshape(1, 1, 2, nev, spins, dil), corr.reshape(1, 1, 2, moms)


def solution(mesh):
    return jax.shard_map(
        functools.partial(body, mesh.shape["snk"]),
        mesh=mesh,
        in_specs=(
            P(("grp", "src"), None, None, None, "snk", None, None),
            P(("grp", "snk"), None, None, None, None),
            P(),
            P(),
        ),
        out_specs=(
            P(("grp", "snk"), "src", None, None, None, None),
            P(("grp", "snk"), "src", None, None),
        ),
        check_vma=False,
    )
```

time: 87.3 us -> 20.7 us (0.24)
  matrix products: 47.7 us -> 0 us
  Pallas kernels: 0 us -> 14.2 us
  between operations: 14.3 us -> 0.65 us
  local copies, waits for them, and re-layouts: 15.1 us -> 5.59 us
  other arithmetic: 5.46 us -> 0 us
  starting transfers between devices: 4.11 us -> 0 us
    dot_general x25 -> x0, matrix products: 47.7 us -> none  [the longest x16 43.9 us: einsum_full(): return jnp.einsum(form, *operands, precision=PRECISE)]
    pallas_call x0 -> x1, Pallas kernels: none -> 14.2 us  [body(): pl.pallas_call(functools.partial(kernel, dims), out_shape=(jax.ShapeDtype...]
    dot_general x2 -> x0, local copies, waits for them, and re-layouts: 4.18 us -> none  [einsum_full(): return jnp.einsum(form, *operands, precision=PRECISE)]
    all_to_all x1 -> x0, starting transfers between devices: 4.11 us -> none  [body(): lax.all_to_all(solutions, 'snk', split_axis=1, concat_axis=4, tiled=True)]
    unnamed x29 -> x13, local copies, waits for them, and re-layouts: 2.09 us -> 5.59 us
    reshape x2 -> x0, local copies, waits for them, and re-layouts: 3.16 us -> none  [the longest x1 1.59 us: correlate(): smear_imag = smear_imag.reshape(4, WINDOW_SITES, 3, 4, NB)]
    add x3 -> x0, local copies, waits for them, and re-layouts: 2.75 us -> none  [the longest x1 1.89 us: correlate(): einsum_full('a,axcsb,axcse->xbe', spin_sign, smear_real, smear_real)]
    sub x3 -> x0, local copies, waits for them, and re-layouts: 2.65 us -> none  [the longest x1 1.78 us: correlate(): einsum_full('a,axcsb,axcse->xbe', spin_sign, smear_real, smear_imag)]
  transfers between devices with their start and end apart: 2 -> 0, of which waited for: 0 -> 0; matrix products, arithmetic and copies ran while one was open for 77% -> 0% of each run, Pallas kernels for 0% -> 0%
where the time goes in v1:
time: 20.7 us; the launch traced here: 20.4 us
  Pallas kernels  14.2 us (69%)
  local copies, waits for them, and re-layouts  5.59 us (27%)
  between operations  0.65 us (3%)
    pallas_call x1, Pallas kernels, body(): pl.pallas_call(functools.partial(kernel, dims), out_shape=(jax.ShapeDtype...  14.2 us
    unnamed x13, local copies, waits for them, and re-layouts  5.59 us

profile of v1, /device:TPU:17, one launch (start us, length us, event | category | flops | bytes accessed | tf_op | source)
XLA Modules:
  0.0 20.4 jit_solution(16454790614837803806)
XLA Ops:
  0.6 0.0 copy-start.4
  0.6 0.7 %copy-done.4 = s32[8,3]{0,1:T(4,128)S(1)} copy-done((s32[8,3]{0,1:T(4,128)S(1)}, s32[8,3]{0,1:T(4,128)}, u32[]{:S(2)}) %copy-start.4) | copy-done | bytes 120
  1.3 0.0 copy-start.3
  1.3 0.1 copy.7.momenta_ref
  1.4 0.6 %copy-done.3 = s32[512]{0:T(512)S(1)} copy-done((s32[512]{0:T(512)S(1)}, s32[512]{0:T(512)}, u32[]{:S(2)}) %copy-start.3) | copy-done | bytes 2072
  2.0 0.0 copy-start
  2.0 1.0 %copy-done = bf16[1,2,64,3,512]{4,2,3,1,0:T(8,128)(2,1)S(1)} copy-done((bf16[1,2,64,3,512]{4,2,3,1,0:T(8,128)(2,1)S(1)}, bf16[1,2,64,3,512]{4,2,3,1,0:T(8,128)(2,1)}, u32[]{:S(2)}) %copy-start) | copy-done | bytes 393240
  3.0 0.0 copy-start.1
  3.0 1.0 %copy-done.1 = bf16[1,4,2,4,16,3,128]{6,4,5,3,2,1,0:T(8,128)(2,1)S(1)} copy-done((bf16[1,4,2,4,16,3,128]{6,4,5,3,2,1,0:T(8,128)(2,1)S(1)}, bf16[1,4,2,4,16,3,128]{6,4,5,3,2,1,0:T(8,128)(2,1)}, u32[]{:S(2)}) %copy-start.1) | copy-done | bytes 393240
  4.0 0.0 copy-start.2
  4.0 0.7 %copy-done.2 = s32[8,384]{1,0:T(8,128)S(1)} copy-done((s32[8,384]{1,0:T(8,128)S(1)}, s32[8,384]{1,0:T(8,128)}, u32[]{:S(2)}) %copy-start.2) | copy-done | bytes 12312
  4.7 14.2 %shard_map.68 = (bf16[4096,128]{1,0:T(8,128)(2,1)S(1)}, f32[2,8]{1,0:T(2,128)S(1)}) custom-call(s32[8,3]{1,0:T(8,128)S(1)} %copy.7.momenta_ref, s32[1,512]{1,0:T(1,128)S(1)} %bitcast.16, s32[8,384]{1,0:T(8,128)S(1)} %copy-done.2, bf16[2,3,4,16,512]{4,3,2,1,0:T(8,128)(2,1)S(1)} %bitcast.14, bf16[4,2,4,48,128]{4,3,2,1,0:T(8,128)(2,1)S(1)} %bitcast.15), custom_call_target="tpu_custom_call" | custom-call | tf_op jit(solution)/shard_map/pallas_call | solution.py:242
  18.9 1.0 %copy.10 = bf16[1,1,2,512,4,128]{5,4,3,2,1,0:T(4,128)(2,1)} copy(bf16[1,1,2,512,4,128]{5,4,3,2,1,0:T(4,128)(2,1)S(1)} %bitcast.13) | data formatting | bytes 2097152
  19.9 0.6 %copy.11 = f32[1,1,2,8]{3,2,1,0:T(2,128)} copy(f32[1,1,2,8]{3,2,1,0:T(2,128)S(1)} %bitcast.17) | data formatting | bytes 128
Async XLA Ops:
  0.6 0.7 %copy-start.4 = (s32[8,3]{0,1:T(4,128)S(1)}, s32[8,3]{0,1:T(4,128)}, u32[]{:S(2)}) copy-start(s32[8,3]{0,1:T(4,128)} %param.7) | copy-start | bytes 292
  1.3 0.7 %copy-start.3 = (s32[512]{0:T(512)S(1)}, s32[512]{0:T(512)}, u32[]{:S(2)}) copy-start(s32[512]{0:T(512)} %param.8) | copy-start | bytes 6148
  2.0 1.0 %copy-start = (bf16[1,2,64,3,512]{4,2,3,1,0:T(8,128)(2,1)S(1)}, bf16[1,2,64,3,512]{4,2,3,1,0:T(8,128)(2,1)}, u32[]{:S(2)}) copy-start(bf16[1,2,64,3,512]{4,2,3,1,0:T(8,128)(2,1)} %param.6) | copy-start | bytes 1179652
  3.0 1.0 %copy-start.1 = (bf16[1,4,2,4,16,3,128]{6,4,5,3,2,1,0:T(8,128)(2,1)S(1)}, bf16[1,4,2,4,16,3,128]{6,4,5,3,2,1,0:T(8,128)(2,1)}, u32[]{:S(2)}) copy-start(bf16[1,4,2,4,16,3,128]{6,4,5,3,2,1,0:T(8,128)(2,1)} %param.5) | copy-start | bytes 1179652
  4.0 0.7 %copy-start.2 = (s32[8,384]{1,0:T(8,128)S(1)}, s32[8,384]{1,0:T(8,128)}, u32[]{:S(2)}) copy-start(s32[8,384]{1,0:T(8,128)} %constant.2.clone.coords_ref) | copy-start | bytes 36868

commit v2 on v1

--- a/solution.py
+++ b/solution.py
@@ -3,7 +3,6 @@
 
 import jax
 import jax.numpy as jnp
-import numpy as np
 from jax import lax
 from jax.experimental import pallas as pl
 from jax.experimental.pallas import tpu as pltpu
@@ -16,17 +15,15 @@
 MESH = pl.DeviceIdType.MESH
 
 
-def site_coordinates(peers, rows, colours, local):
-    table = np.zeros((8, peers, rows), np.int32)
-    for owner in range(peers):
-        for colour in range(colours):
-            site = owner * local + np.arange(local)
-            here = slice(colour * local, (colour + 1) * local)
-            table[0, owner, here] = site % LAT
-            table[1, owner, here] = site // LAT % LAT
-            table[2, owner, here] = site // (LAT * LAT)
-    table = table.reshape(8, peers * rows)
-    return np.concatenate([table, table], axis=1)
+def coordinates(peers, rows, local):
+    total = peers * rows
+    lane = lax.broadcasted_iota(jnp.int32, (1, 2 * total), 1)
+    lane = jnp.where(lane >= total, lane - total, lane)
+    owner = sum((lane >= j * rows).astype(jnp.int32) for j in range(1, peers))
+    site = owner * local + lax.rem(lane - owner * rows, jnp.int32(local))
+    x = lax.rem(site, jnp.int32(LAT))
+    y = lax.rem(lax.div(site, jnp.int32(LAT)), jnp.int32(LAT))
+    return x, y, lax.div(site, jnp.int32(LAT * LAT))
 
 
 def split(values):
@@ -35,9 +32,9 @@
 
 
 def kernel(
-    dims, momenta_ref, ordering_ref, coords_ref, eig_hbm, sol_hbm, peramb_ref, corr_ref,
-    eig, eig_t, sol, pairs, fac_own, fac_got, table, weights,
-    eig_sem, sol_sem, send_sem, recv_sem, fac_send, fac_recv,
+    dims, momenta_hbm, ordering_hbm, eig_hbm, sol_hbm, peramb_ref, corr_ref,
+    momenta_ref, ordering_ref, eig, eig_t, sol, pairs, fac_own, fac_got, table, weights,
+    small_sem, eig_sem, sol_sem, send_sem, recv_sem, fac_send, fac_recv,
 ):
     peers, spins, rows, local, colours, nev, dil, moms, direct, scale = dims
     total = peers * rows
@@ -60,7 +57,11 @@
         pltpu.make_async_copy(sol_hbm.at[me, :, a], sol.at[a, :, me], sol_sem.at[a])
         for a in range(spins)
     ]
-    for copy in eig_copies + own_copies:
+    small_copies = [
+        pltpu.make_async_copy(momenta_hbm, momenta_ref, small_sem.at[0]),
+        pltpu.make_async_copy(ordering_hbm, ordering_ref, small_sem.at[1]),
+    ]
+    for copy in small_copies + eig_copies + own_copies:
         copy.start()
 
     barrier = pltpu.get_barrier_semaphore()
@@ -84,7 +85,7 @@
             copy.start()
             sends.append(copy)
 
-    for copy in eig_copies:
+    for copy in small_copies + eig_copies:
         copy.wait()
     vectors = eig[...].reshape(2 * total, nev)
     block_of = lax.div(ordering_ref[...], jnp.int32(nev // NB))
@@ -114,12 +115,12 @@
 
     eig_t[...] = vectors.astype(jnp.float32).T.astype(jnp.bfloat16)
 
-    mom = [jnp.zeros((moms, 2 * total), jnp.int32) for _ in range(3)]
-    which = lax.broadcasted_iota(jnp.int32, (moms, 2 * total), 0)
-    for i in range(3):
-        for p in range(moms):
-            mom[i] = jnp.where(which == p, momenta_ref[p, i], mom[i])
-    turns = sum(mom[i] * coords_ref[i : i + 1, :] for i in range(3))
+    square = (moms, moms)
+    eye = lax.broadcasted_iota(jnp.int32, square, 0) == lax.broadcasted_iota(jnp.int32, square, 1)
+    turns = jnp.zeros((moms, 2 * total), jnp.int32)
+    for i, place in enumerate(coordinates(peers, rows, local)):
+        column = jnp.sum(jnp.where(eye, momenta_ref[i : i + 1, :], 0), axis=1, keepdims=True)
+        turns = turns + column * place
     turns = jnp.bitwise_and(turns + LAT // 2, LAT - 1) - LAT // 2
     angle = turns.astype(jnp.float32) * (2.0 * math.pi / LAT)
     phases = jnp.concatenate([jnp.cos(angle), jnp.sin(angle)], axis=0)
@@ -201,8 +202,6 @@
     sum_cos, sum_sin = summed[:moms], summed[moms:]
     real = jnp.sum(at_cos * sum_cos + at_sin * sum_sin, axis=1, keepdims=True)
     imag = jnp.sum(at_sin * sum_cos - at_cos * sum_sin, axis=1, keepdims=True)
-    square = (moms, moms)
-    eye = lax.broadcasted_iota(jnp.int32, square, 0) == lax.broadcasted_iota(jnp.int32, square, 1)
     out = [
         jnp.sum(jnp.where(eye, column, 0.0), axis=0, keepdims=True) * scale
         for column in (real, imag)
@@ -234,9 +233,9 @@
         sol = jnp.pad(sol, pad)
         eig = jnp.transpose(eig, (0, 2, 1, 3, 4)).reshape(2, peers, used, nev)
         eig = jnp.pad(eig, pad[1:])
-    coords = jnp.asarray(site_coordinates(peers, rows, colours, local))
     scale = 1.0 / (sites * NB)
 
+    operands = (momenta.T, ordering.reshape(1, nev), eig, sol)
     vmem = pl.BlockSpec(memory_space=pltpu.VMEM)
     dims = (peers, spins, rows, local, colours, nev, dil, moms, direct, scale)
     peramb, corr = pl.pallas_call(
@@ -245,15 +244,11 @@
             jax.ShapeDtypeStruct((2 * nev * spins, dil), jnp.bfloat16),
             jax.ShapeDtypeStruct((2, moms), jnp.float32),
         ),
-        in_specs=[
-            pl.BlockSpec(memory_space=pltpu.SMEM),
-            vmem,
-            vmem,
-            pl.BlockSpec(memory_space=pl.ANY),
-            pl.BlockSpec(memory_space=pl.ANY),
-        ],
+        in_specs=[pl.BlockSpec(memory_space=pltpu.HBM)] * 4,
         out_specs=(vmem, vmem),
         scratch_shapes=[
+            pltpu.VMEM((3, moms), jnp.int32),
+            pltpu.VMEM((1, nev), jnp.int32),
             pltpu.VMEM((2, peers, rows, nev), jnp.bfloat16),
             pltpu.VMEM((nev, 2 * total), jnp.bfloat16),
             pltpu.VMEM((spins, 2, peers, rows, dil), jnp.bfloat16),
@@ -262,6 +257,7 @@
             pltpu.VMEM((NB, 2 * total), jnp.float32),
             pltpu.VMEM((2 * total, 6 * NB), jnp.bfloat16),
             pltpu.VMEM((2 * total, total), jnp.float32),
+            pltpu.SemaphoreType.DMA((2,)),
             pltpu.SemaphoreType.DMA((peers * colours,)),
             pltpu.SemaphoreType.DMA((spins,)),
             pltpu.SemaphoreType.DMA((spins, peers)),
@@ -272,7 +268,7 @@
         compiler_params=pltpu.CompilerParams(
             collective_id=0, has_side_effects=True, vmem_limit_bytes=40 * 1024 * 1024
         ),
-    )(momenta, ordering.reshape(1, nev), coords, eig, sol)
+    )(*(pltpu.with_memory_space_constraint(v, pltpu.HBM) for v in operands))
     return peramb.reshape(1, 1, 2, nev, spins, dil), corr.reshape(1, 1, 2, moms)
 
 

time: 20.7 us -> 15.9 us (0.77)
  local copies, waits for them, and re-layouts: 5.59 us -> 1.53 us
  Pallas kernels: 14.2 us -> 13.5 us
    unnamed x13 -> x2, local copies, waits for them, and re-layouts: 5.59 us -> 1.53 us
    pallas_call x1, Pallas kernels: 14.2 us -> 13.5 us  [body(): pl.pallas_call(functools.partial(kernel, dims), out_shape=(jax.ShapeDtype...]
where the time goes in v2:
time: 15.9 us; the launch traced here: 15.7 us
  Pallas kernels  13.5 us (85%)
  local copies, waits for them, and re-layouts  1.53 us (10%)
  between operations  0.64 us (4%)
    pallas_call x1, Pallas kernels, body(): pl.pallas_call(functools.partial(kernel, dims), out_shape=(jax.ShapeDtype...  13.5 us
    unnamed x2, local copies, waits for them, and re-layouts  1.53 us

profile of v2, /device:TPU:17, one launch (start us, length us, event | category | flops | bytes accessed | tf_op | source)
XLA Modules:
  0.0 15.7 jit_solution(12152850728416910972)
XLA Ops:
  0.6 13.5 %shard_map.59 = (bf16[4096,128]{1,0:T(8,128)(2,1)S(1)}, f32[2,8]{1,0:T(2,128)S(1)}) custom-call(s32[3,8]{1,0:T(4,128)} %bitcast.18, s32[1,512]{1,0:T(1,128)} %bitcast.19, bf16[2,3,4,16,512]{4,3,2,1,0:T(8,128)(2,1)} %bitcast.16, bf16[4,2,4,48,128]{4,3,2,1,0:T(8,128)(2,1)} %bitcast.17), custom_call_target="tpu_custom_call" | custom-call | tf_op jit(solution)/shard_map/pallas_call | solution.py:241
  14.2 1.0 %copy.8 = bf16[1,1,2,512,4,128]{5,4,3,2,1,0:T(4,128)(2,1)} copy(bf16[1,1,2,512,4,128]{5,4,3,2,1,0:T(4,128)(2,1)S(1)} %bitcast.14) | data formatting | bytes 2097152
  15.2 0.6 %copy.9 = f32[1,1,2,8]{3,2,1,0:T(2,128)} copy(f32[1,1,2,8]{3,2,1,0:T(2,128)S(1)} %bitcast.15) | data formatting | bytes 128

commit v3 on v2

--- a/solution.py
+++ b/solution.py
@@ -10,6 +10,7 @@
 
 LAT = 64
 NB = 32
+AHEAD = 3
 SPIN_SIGNS = (1.0, 1.0, -1.0, -1.0)
 EXACT = lax.Precision.HIGHEST
 MESH = pl.DeviceIdType.MESH
@@ -82,8 +83,14 @@
                 device_id={"snk": other},
                 device_id_type=MESH,
             )
+            sends.append(copy)
+
+    def spin_sends(a):
+        return sends[a * (peers - 1) : (a + 1) * (peers - 1)]
+
+    for a in range(min(AHEAD, spins)):
+        for copy in spin_sends(a):
             copy.start()
-            sends.append(copy)
 
     for copy in small_copies + eig_copies:
         copy.wait()
@@ -127,8 +134,13 @@
 
     def smear(a):
         own_copies[a].wait()
-        for copy in sends[a * (peers - 1) : (a + 1) * (peers - 1)]:
+        for copy in spin_sends(a):
             copy.wait_recv()
+        for copy in spin_sends(a):
+            copy.wait_send()
+        if a + AHEAD < spins:
+            for copy in spin_sends(a + AHEAD):
+                copy.start()
         s_real = sol[a, 0].reshape(total, dil)
         s_imag = sol[a, 1].reshape(total, dil)
         right = jnp.concatenate(
@@ -208,13 +220,26 @@
     ]
     corr_ref[...] = jnp.concatenate(out, axis=0)
 
-    for copy in sends:
-        copy.wait_send()
-
     @pl.when(me == source)
     def _():
         for copy in fac_sends:
             copy.wait_send()
+
+
+def write_out(peramb, corr, peramb_hbm, corr_hbm, sems):
+    pieces = sems.shape[0] - 1
+    depth = peramb.shape[0] // pieces
+    copies = [
+        pltpu.make_async_copy(
+            peramb.at[pl.ds(i * depth, depth)], peramb_hbm.at[pl.ds(i * depth, depth)], sems.at[i]
+        )
+        for i in range(pieces)
+    ]
+    copies.append(pltpu.make_async_copy(corr, corr_hbm, sems.at[pieces]))
+    for copy in copies:
+        copy.start()
+    for copy in copies:
+        copy.wait()
 
 
 def body(peers, solutions, eigvecs, momenta, ordering):
@@ -269,6 +294,17 @@
             collective_id=0, has_side_effects=True, vmem_limit_bytes=40 * 1024 * 1024
         ),
     )(*(pltpu.with_memory_space_constraint(v, pltpu.HBM) for v in operands))
+    hbm = pl.BlockSpec(memory_space=pltpu.HBM)
+    peramb, corr = pl.pallas_call(
+        write_out,
+        out_shape=(
+            jax.ShapeDtypeStruct(peramb.shape, peramb.dtype),
+            jax.ShapeDtypeStruct(corr.shape, corr.dtype),
+        ),
+        in_specs=[vmem, vmem],
+        out_specs=(hbm, hbm),
+        scratch_shapes=[pltpu.SemaphoreType.DMA((5,))],
+    )(*(pltpu.with_memory_space_constraint(v, pltpu.VMEM) for v in (peramb, corr)))
     return peramb.reshape(1, 1, 2, nev, spins, dil), corr.reshape(1, 1, 2, moms)
 
 

time: 15.9 us -> 14.8 us (0.931)
  local copies, waits for them, and re-layouts: 1.53 us -> 0 us
  Pallas kernels: 13.5 us -> 14 us
    unnamed x2 -> x0, local copies, waits for them, and re-layouts: 1.53 us -> none
    pallas_call x0 -> x1, Pallas kernels: none -> 1.01 us  [body(): pl.pallas_call(write_out, out_shape=(jax.ShapeDtypeStruct(peramb.shape, p...]
    pallas_call x1, Pallas kernels: 13.5 us -> 13 us  [body(): pl.pallas_call(functools.partial(kernel, dims), out_shape=(jax.ShapeDtype...]
where the time goes in v3:
time: 14.8 us; the launch traced here: 14.7 us
  Pallas kernels  14 us (95%)
  between operations  0.64 us (4%)
    pallas_call x1, Pallas kernels, body(): pl.pallas_call(functools.partial(kernel, dims), out_shape=(jax.ShapeDtype...  13 us
    pallas_call x1, Pallas kernels, body(): pl.pallas_call(write_out, out_shape=(jax.ShapeDtypeStruct(peramb.shape, p...  1.01 us

profile of v3, /device:TPU:17, one launch (start us, length us, event | category | flops | bytes accessed | tf_op | source)
XLA Modules:
  0.0 14.7 jit_solution(6674209190864543535)
XLA Ops:
  0.6 13.0 %shard_map.59 = (bf16[4096,128]{1,0:T(8,128)(2,1)S(1)}, f32[2,8]{1,0:T(2,128)S(1)}) custom-call(s32[3,8]{1,0:T(4,128)} %bitcast.16, s32[1,512]{1,0:T(1,128)} %bitcast.17, bf16[2,3,4,16,512]{4,3,2,1,0:T(8,128)(2,1)} %bitcast.14, bf16[4,2,4,48,128]{4,3,2,1,0:T(8,128)(2,1)} %bitcast.15), custom_call_target="tpu_custom_call" | custom-call | tf_op jit(solution)/shard_map/pallas_call | solution.py:266
  13.7 1.0 %shard_map.60 = (bf16[4096,128]{1,0:T(8,128)(2,1)}, f32[2,8]{1,0:T(2,128)}) custom-call(bf16[4096,128]{1,0:T(8,128)(2,1)S(1)} %get-tuple-element.6.peramb, f32[2,8]{1,0:T(2,128)S(1)} %get-tuple-element.7.corr), custom_call_target="tpu_custom_call" | custom-call | tf_op jit(solution)/shard_map/pallas_call | solution.py:298
